TPU v7x, 256 devices: a whole 4x4x8 slice. The times are simulated.
256 devices in a mesh: expert: 32 (over z, y_lo, core), tensor: 8 (over y_hi, x).
Axes of the slice: x: 4, y: 4 (y_hi: 2, y_lo: 2; y = y_hi * 2 + y_lo), z: 8, core: 2. Of those that a mesh axis runs over, the one named last changes fastest.
Arguments:
- tokens: bfloat16 [2048, 7168], P('expert', 'tensor'), may hold values from -6 to 6
- layer_output_gradient: bfloat16 [2048, 7168], P('expert', 'tensor'), may hold values from -6 to 6
- routes: int32 [2048, 2], P('expert'), may hold values from 0 to 31, all different within a row; in each aligned block of 64 rows (0 to 63, 64 to 127, ...) at most 8 rows name the same one
- router_weight_pair: float32 [2048, 2], P('expert'), may hold values from 0.05 to 1
- gating_projection: bfloat16 [32, 7168, 2432], P('expert', None, 'tensor'), may hold values from -0.0625 to 0.0625
- expanding_projection: bfloat16 [32, 7168, 2432], P('expert', None, 'tensor'), may hold values from -0.0625 to 0.0625
- contracting_projection: bfloat16 [32, 2432, 7168], P('expert', 'tensor'), may hold values from -0.125 to 0.125
- leading_correction_matrix: bfloat16 [32, 2432, 16], P('expert', 'tensor'), may hold values from -0.125 to 0.125
- trailing_correction_matrix: bfloat16 [32, 16, 7168], P('expert', None, 'tensor'), may hold values from -0.0625 to 0.0625
Outputs:
- source_derivative: bfloat16 [2048, 7168], P('expert', 'tensor')
- leading_correction_derivative: float32 [32, 2432, 16], P('expert', 'tensor')
- trailing_correction_derivative: float32 [32, 16, 7168], P('expert', None, 'tensor')
Inputs may be any that keep to these rules, and one draw needn't show every extreme that they name: `routes`: among the 64 tokens of one index of expert no expert is named by more than 8 assignments, a bound that some block reaches.
All inputs are finite; a program needn't handle non-finite values.
Results may differ from a plain program's by a relative error of at most 0.019.
Values may be sent and summed in bfloat16 or wider, within the bound.
A program may use at most 128 MiB of HBM per device.

v0:
```python
import jax
import jax.numpy as jnp
from jax import lax
from jax.sharding import PartitionSpec as P

EXP_DEV = 1
CSRC = 8


correction_multiplier = 2.0


def on_device(
    tokens,
    layer_output_gradient,
    routes,
    router_weight_pair,
    gating_projection,
    expanding_projection,
    contracting_projection,
    leading_correction_matrix,
    trailing_correction_matrix,
):
    groups = lax.axis_size("expert")
    experts = EXP_DEV * groups
    width_local = tokens.shape[1]
    flat = routes.reshape(-1)
    onehot = (flat[:, None] == jnp.arange(experts, dtype=jnp.int32)[None, :]).astype(jnp.int32)
    earlier = jnp.cumsum(onehot, axis=0) - onehot
    slots = jnp.sum(earlier * onehot, axis=1)
    dest = flat * CSRC + slots
    total = experts * CSRC
    column_start = lax.axis_index("tensor") * width_local

    def place(values):
        return jnp.zeros((total, values.shape[1]), jnp.bfloat16).at[dest].set(values)

    def to_experts(buffer):
        width = buffer.shape[1]
        sectioned = buffer.reshape(groups, EXP_DEV, CSRC, width)
        return jnp.transpose(sectioned, (1, 0, 2, 3)).reshape(EXP_DEV, groups * CSRC, width)

    full_tokens, full_grad = (
        lax.all_gather(tokens, "tensor", axis=1, tiled=True),
        lax.all_gather(layer_output_gradient, "tensor", axis=1, tiled=True),
    )
    x_buf = place(jnp.repeat(full_tokens, 2, axis=0))
    scaled = router_weight_pair[:, :, None] * full_grad[:, None, :].astype(jnp.float32)
    g_buf = place(scaled.astype(jnp.bfloat16).reshape(-1, full_grad.shape[1]))
    x_recv, g_recv = (
        lax.all_to_all(x_buf, "expert", split_axis=0, concat_axis=0, tiled=True),
        lax.all_to_all(g_buf, "expert", split_axis=0, concat_axis=0, tiled=True),
    )
    x_rows = to_experts(x_recv)
    output_grad_rows = to_experts(g_recv)
    target_derivative_portion = lax.dynamic_slice_in_dim(
        output_grad_rows, column_start, width_local, 2
    )
    gate = jnp.einsum("erd,edf->erf", x_rows, gating_projection, preferred_element_type=jnp.float32)
    up = jnp.einsum(
        "erd,edf->erf", x_rows, expanding_projection, preferred_element_type=jnp.float32
    )
    sig = jax.nn.sigmoid(gate)
    act = gate * sig
    hidden_units = (act * up).astype(jnp.bfloat16)
    lowrank_partial = jnp.einsum(
        "taw,twy->tay", hidden_units, leading_correction_matrix, preferred_element_type=jnp.float32
    )
    probe_partial = jnp.einsum(
        "foh,frh->for",
        target_derivative_portion,
        trailing_correction_matrix,
        preferred_element_type=jnp.float32,
    )
    low_sum, probe_sum = (
        lax.psum(lowrank_partial.astype(jnp.bfloat16), "tensor").astype(jnp.float32),
        lax.psum(probe_partial.astype(jnp.bfloat16), "tensor").astype(jnp.float32),
    )
    lowrank_rows = low_sum.astype(jnp.bfloat16)
    probe_vector = probe_sum.astype(jnp.bfloat16)
    hidden_gradient = jnp.einsum(
        "erd,efd->erf", output_grad_rows, contracting_projection, preferred_element_type=jnp.float32
    )
    hidden_gradient = hidden_gradient + correction_multiplier * jnp.einsum(
        "lyp,ljp->lyj", probe_vector, leading_correction_matrix, preferred_element_type=jnp.float32
    )
    dgate = (hidden_gradient * up * sig * (1.0 + gate * (1.0 - sig))).astype(jnp.bfloat16)
    dup = (hidden_gradient * act).astype(jnp.bfloat16)
    leading_correction_derivative = correction_multiplier * jnp.einsum(
        "erf,erk->efk", hidden_units, probe_vector, preferred_element_type=jnp.float32
    )
    trailing_correction_derivative = correction_multiplier * jnp.einsum(
        "erk,erd->ekd", lowrank_rows, target_derivative_portion, preferred_element_type=jnp.float32
    )
    dx_part = jnp.einsum(
        "erf,edf->erd", dgate, gating_projection, preferred_element_type=jnp.float32
    )
    dx_part = dx_part + jnp.einsum(
        "erf,edf->erd", dup, expanding_projection, preferred_element_type=jnp.float32
    )
    summed = lax.psum_scatter(
        dx_part.astype(jnp.bfloat16), "tensor", scatter_dimension=2, tiled=True
    ).astype(jnp.float32)
    width = summed.shape[2]
    sectioned = summed.reshape(EXP_DEV, groups, CSRC, width)
    returned = lax.all_to_all(
        jnp.transpose(sectioned, (1, 0, 2, 3)).reshape(total, width).astype(jnp.bfloat16),
        "expert",
        split_axis=0,
        concat_axis=0,
        tiled=True,
    ).astype(jnp.float32)
    picked = returned[dest].reshape(-1, 2, width_local)
    source_derivative = (picked[:, 0] + picked[:, 1]).astype(jnp.bfloat16)
    return (source_derivative, leading_correction_derivative, trailing_correction_derivative)


def solution(mesh):
    placed = (
        P("expert", "tensor"),
        P("expert", "tensor"),
        P("expert", None),
        P("expert", None),
        P("expert", None, "tensor"),
        P("expert", None, "tensor"),
        P("expert", "tensor", None),
        P("expert", "tensor", None),
        P("expert", None, "tensor"),
    )
    return jax.shard_map(
        on_device,
        mesh=mesh,
        in_specs=placed,
        out_specs=(P("expert", "tensor"), P("expert", "tensor", None), P("expert", None, "tensor")),
        check_vma=False,
    )
```

profile of v0, /device:TPU:1, one launch (start us, length us, event | category | flops | bytes accessed | tf_op | source)
XLA Modules:
  0.0 434.1 jit_solution(16263925273366446662)
XLA Ops:
  9.5 32.0 %all_gather.7 = bf16[64,7168]{1,0:T(8,128)(2,1)S(1)} all-gather(bf16[64,896]{1,0:T(8,128)(2,1)} %param.9), channel_id=1, replica_groups=mesh['expert'=32,'tensor'=8] {'tensor'}, dimensions={1}, use_global_device_ids=true | all-gather | bytes 1032192 | tf_op jit(solution)/shard_map/all_gather | solution.py:44
  42.4 1.7 reshape.175
  44.1 6.4 %scatter_custom_fusion.1 = bf16[256,7168]{1,0:T(8,128)(2,1)} fusion(s32[128]{0:T(128)S(1)} %fusion.32, bf16[128,7168]{1,0:T(8,128)(2,1)} %reshape.175, bf16[]{:T(256)} %constant.9.clone.1), kind=kCustom, calls=%fused_computation.21 | custom fusion | bytes 3670528 | tf_op jit(solution)/shard_map/scatter | solution.py:36
  50.5 15.5 %all-to-all-start.1 = ((bf16[32,8,7168]{2,1,0:T(8,128)(2,1)}), bf16[32,8,7168]{2,1,0:T(8,128)(2,1)}, u32[]{:S(2)}, u32[]{:S(2)}) async-start(bf16[32,8,7168]{2,1,0:T(8,128)(2,1)} %bitcast.68), calls=%async_computation.1 | async-start | bytes 7340032 | tf_op jit(solution)/shard_map/all_to_all | solution.py:51
  66.3 32.9 %all_gather.6 = bf16[64,7168]{1,0:T(8,128)(2,1)S(1)} all-gather(bf16[64,896]{1,0:T(8,128)(2,1)S(1)} %copy-done.2), channel_id=1, replica_groups=mesh['expert'=32,'tensor'=8] {'tensor'}, dimensions={1}, use_global_device_ids=true | all-gather | bytes 1032192 | tf_op jit(solution)/shard_map/all_gather | solution.py:45
  99.1 2.8 mul.99
  101.9 5.6 %mul.100 = f32[128,7168]{1,0:T(8,128)} reshape(f32[64,2,7168]{2,1,0:T(2,128)} %mul.99) | data formatting | bytes 7340032 | tf_op jit(solution)/shard_map/mul | solution.py:48
  107.6 7.0 %scatter_custom_fusion = bf16[256,7168]{1,0:T(8,128)(2,1)} fusion(s32[128]{0:T(128)S(1)} %fusion.32, f32[128,7168]{1,0:T(8,128)} %mul.100, f32[128]{0:T(128)S(1)} %mul.97, bf16[]{:T(256)} %constant.9.clone.1), kind=kCustom, calls=%fused_computation.19 | custom fusion | flops 1835008 | bytes 7340546 | tf_op jit(solution)/shard_map/scatter | solution.py:36
  114.6 35.0 %all-to-all-done.1 = bf16[32,8,7168]{2,1,0:T(8,128)(2,1)} async-done(((bf16[32,8,7168]{2,1,0:T(8,128)(2,1)}), bf16[32,8,7168]{2,1,0:T(8,128)(2,1)}, u32[]{:S(2)}, u32[]{:S(2)}) %all-to-all-start.1) | async-done | bytes 3670048 | tf_op jit(solution)/shard_map/all_to_all | solution.py:51
  149.6 5.9 %all-to-all-start = ((bf16[32,8,7168]{2,1,0:T(8,128)(2,1)}), bf16[32,8,7168]{2,1,0:T(8,128)(2,1)}, u32[]{:S(2)}, u32[]{:S(2)}) async-start(bf16[32,8,7168]{2,1,0:T(8,128)(2,1)} %bitcast.67), calls=%async_computation | async-start | bytes 7340032 | tf_op jit(solution)/shard_map/all_to_all | solution.py:52
  155.6 4.8 %fusion.4 = f32[256,304]{0,1:T(8,128)S(1)} fusion(bf16[1,7168,304]{1,2,0:T(8,128)(2,1)} %param.13, bf16[32,8,7168]{2,1,0:T(8,128)(2,1)} %all-to-all-done.1), kind=kOutput, calls=%fused_computation.8 | convolution fusion | flops 1115684864 | bytes 8339456 | tf_op jit(solution)/shard_map/erd,edf->erf/dot_general | solution.py:59
  160.4 3.4 multiply_convert_fusion.2
  164.0 76.9 %all-to-all-done = bf16[32,8,7168]{2,1,0:T(8,128)(2,1)} async-done(((bf16[32,8,7168]{2,1,0:T(8,128)(2,1)}), bf16[32,8,7168]{2,1,0:T(8,128)(2,1)}, u32[]{:S(2)}, u32[]{:S(2)}) %all-to-all-start) | async-done | bytes 3670048 | tf_op jit(solution)/shard_map/all_to_all | solution.py:52
  242.1 36.1 %all-reduce = (bf16[256,16]{0,1:T(8,128)(2,1)S(1)}, bf16[256,16]{0,1:T(8,128)(2,1)S(1)}) all-reduce(bf16[256,16]{0,1:T(8,128)(2,1)S(1)} %convolution_convert_fusion.1, bf16[256,16]{0,1:T(8,128)(2,1)S(1)} %convolution_convert_fusion), channel_id=1, replica_groups=mesh['expert'=32,'tensor'=8] {'tensor'}, use_global_device_ids=true, to_apply=%region_3.4 | all-reduce | flops 8192 | bytes 32768 | tf_op jit(solution)/shard_map/psum | solution.py:77
  278.2 4.8 %fusion.9 = f32[256,304]{0,1:T(8,128)S(1)} fusion(bf16[1,304,7168]{2,1,0:T(8,128)(2,1)} %param.15, bf16[32,8,7168]{2,1,0:T(8,128)(2,1)} %all-to-all-done), kind=kOutput, calls=%fused_computation.13 | convolution fusion | flops 1115684864 | bytes 8339456 | tf_op jit(solution)/shard_map/erd,efd->erf/dot_general | solution.py:81
  283.3 2.2 fusion.2
  285.5 4.2 fusion.1
  289.8 16.3 %copy.27 = bf16[1,256,7168]{1,0,2:T(2,128)(2,1)} copy(bf16[1,256,7168]{2,1,0:T(8,128)(2,1)} %fusion.1) | data formatting | bytes 7340032
  306.1 5.6 %copy.41 = bf16[7168,1,256]{2,0,1:T(8,128)(2,1)} copy(bf16[7168,1,256]{2,1,0:T(2,128)(2,1)} %bitcast.66) | data formatting | bytes 7340032
  311.7 84.9 %reduce-scatter.4.cloned.1.call-done = bf16[896,256]{1,0:T(8,128)(2,1)} async-done(((bf16[7168,256]{1,0:T(8,128)(2,1)}), bf16[896,256]{1,0:T(8,128)(2,1)}) %reduce-scatter.4.cloned.1.call-update) | async-done | bytes 458768
  398.1 2.4 copy.28
  400.5 9.3 %all-to-all-start.2 = ((bf16[32,8,896]{2,1,0:T(8,128)(2,1)}), bf16[32,8,896]{2,1,0:T(8,128)(2,1)S(1)}, u32[]{:S(2)}, u32[]{:S(2)}) async-start(bf16[32,8,896]{2,1,0:T(8,128)(2,1)} %bitcast.12), calls=%async_computation.2 | async-start | bytes 917504 | tf_op jit(solution)/shard_map/all_to_all | solution.py:106
  409.9 1.8 fusion.19
  412.5 12.6 %all-to-all-done.2 = bf16[32,8,896]{2,1,0:T(8,128)(2,1)S(1)} async-done(((bf16[32,8,896]{2,1,0:T(8,128)(2,1)}), bf16[32,8,896]{2,1,0:T(8,128)(2,1)S(1)}, u32[]{:S(2)}, u32[]{:S(2)}) %all-to-all-start.2) | async-done | bytes 458784 | tf_op jit(solution)/shard_map/all_to_all | solution.py:106
  (50 shorter events, 9.6 us)
Async XLA Ops:
  7.2 233.8 %copy-start = (bf16[1,16,896]{2,1,0:T(8,128)(2,1)S(1)}, bf16[1,16,896]{2,1,0:T(8,128)(2,1)}, u32[]{:S(2)}) copy-start(bf16[1,16,896]{2,1,0:T(8,128)(2,1)} %param.17) | copy-start | bytes 86020
  50.5 15.5 %copy-start.4 = (f32[64,2]{0,1:T(2,128)S(1)}, f32[64,2]{0,1:T(2,128)}, u32[]{:S(2)}) copy-start(f32[64,2]{0,1:T(2,128)} %param.12) | copy-start | bytes 1540
  50.5 15.8 %copy-start.2 = (bf16[64,896]{1,0:T(8,128)(2,1)S(1)}, bf16[64,896]{1,0:T(8,128)(2,1)}, u32[]{:S(2)}) copy-start(bf16[64,896]{1,0:T(8,128)(2,1)} %param.10) | copy-start | bytes 344068
  50.5 99.1 %all-to-all-start.1 = ((bf16[32,8,7168]{2,1,0:T(8,128)(2,1)}), bf16[32,8,7168]{2,1,0:T(8,128)(2,1)}, u32[]{:S(2)}, u32[]{:S(2)}) async-start(bf16[32,8,7168]{2,1,0:T(8,128)(2,1)} %bitcast.68), calls=%async_computation.1 | async-start | bytes 7340032 | tf_op jit(solution)/shard_map/all_to_all | solution.py:51
  149.6 10.8 %slice-start.2 = ((s8[4358144]{0:T(1024)(128)(4,1)}), s8[163840]{0:T(1024)(128)(4,1)S(1)}, s32[]{:S(2)}) async-start(s8[4358144]{0:T(1024)(128)(4,1)} %bitcast.72), calls=%async_computation.7 | async-start | bytes 327680
  149.6 91.3 %all-to-all-start = ((bf16[32,8,7168]{2,1,0:T(8,128)(2,1)}), bf16[32,8,7168]{2,1,0:T(8,128)(2,1)}, u32[]{:S(2)}, u32[]{:S(2)}) async-start(bf16[32,8,7168]{2,1,0:T(8,128)(2,1)} %bitcast.67), calls=%async_computation | async-start | bytes 7340032 | tf_op jit(solution)/shard_map/all_to_all | solution.py:52
  155.5 241.1 %reduce-scatter.4.cloned.1.call-start = ((), (), s32[]{:S(2)}) async-start(), calls=%async_computation.4 | async-start | bytes 4128768
  155.6 4.8 %slice-start.3 = ((s8[4358144]{0:T(1024)(128)(4,1)}), s8[4194304]{0:T(1024)(128)(4,1)S(1)}, s32[]{:S(2)}) async-start(s8[4358144]{0:T(1024)(128)(4,1)} %bitcast.72), calls=%async_computation.8 | async-start | bytes 8388608
  160.4 3.4 copy-start.3
  242.1 41.2 %slice-start = ((s8[4358144]{0:T(1024)(128)(4,1)}), s8[163840]{0:T(1024)(128)(4,1)S(1)}, s32[]{:S(2)}) async-start(s8[4358144]{0:T(1024)(128)(4,1)} %bitcast.70), calls=%async_computation.5 | async-start | bytes 327680
  278.2 5.1 %slice-start.1 = ((s8[4358144]{0:T(1024)(128)(4,1)}), s8[4194304]{0:T(1024)(128)(4,1)S(1)}, s32[]{:S(2)}) async-start(s8[4358144]{0:T(1024)(128)(4,1)} %bitcast.70), calls=%async_computation.6 | async-start | bytes 8388608
  278.2 7.3 %slice-start.4 = ((s8[4358144]{0:T(1024)(128)(4,1)}), s8[4194304]{0:T(1024)(128)(4,1)S(1)}, s32[]{:S(2)}) async-start(s8[4358144]{0:T(1024)(128)(4,1)} %bitcast.74), calls=%async_computation.9 | async-start | bytes 8388608
  283.3 2.2 slice-start.5
  400.5 24.6 %all-to-all-start.2 = ((bf16[32,8,896]{2,1,0:T(8,128)(2,1)}), bf16[32,8,896]{2,1,0:T(8,128)(2,1)S(1)}, u32[]{:S(2)}, u32[]{:S(2)}) async-start(bf16[32,8,896]{2,1,0:T(8,128)(2,1)} %bitcast.12), calls=%async_computation.2 | async-start | bytes 917504 | tf_op jit(solution)/shard_map/all_to_all | solution.py:106
  411.7 15.6 %copy-start.1 = (bf16[1,16,896]{2,1,0:T(8,128)(2,1)S(1)}, bf16[1,16,896]{2,1,0:T(8,128)(2,1)}, u32[]{:S(2)}) copy-start(bf16[1,16,896]{2,1,0:T(8,128)(2,1)} %param.17) | copy-start | bytes 86020
Sparse Core Ops, SparseCore 0:
  311.8 84.7 reduce-scatter.3
where the time goes:
time: 435 us; the launch traced here: 434 us
  waiting for transfers between devices  209 us (48%)
  blocking collectives  101 us (23%)
  local copies, waits for them, and re-layouts  46.1 us (11%)
  starting transfers between devices  30.8 us (7%)
  matrix products  23.6 us (5%)
  between operations  14.3 us (3%)
  other arithmetic  8.88 us (2%)
    unnamed x2, waiting for transfers between devices  84.9 us
    all_to_all x1, waiting for transfers between devices, on_device(): lax.all_to_all(g_buf, 'expert', split_axis=0, concat_axis=0, tiled=True)  76.9 us
    psum x1, blocking collectives, on_device(): lax.psum(probe_partial.astype(jnp.bfloat16), 'tensor').astype(jnp.float32)  36.1 us
    all_to_all x1, waiting for transfers between devices, on_device(): lax.all_to_all(x_buf, 'expert', split_axis=0, concat_axis=0, tiled=True)  35 us
    all_gather x1, blocking collectives, on_device(): lax.all_gather(layer_output_gradient, 'tensor', axis=1, tiled=True)  32.9 us
    all_gather x1, blocking collectives, on_device(): lax.all_gather(tokens, 'tensor', axis=1, tiled=True)  32 us
    unnamed x28, local copies, waits for them, and re-layouts  26.7 us
    all_to_all x1, starting transfers between devices, on_device(): lax.all_to_all(x_buf, 'expert', split_axis=0, concat_axis=0, tiled=True)  15.5 us
  transfers between devices with their start and end apart: 4, of which 4 were waited for; matrix products, arithmetic and copies ran while one was open for 6% of the time, Pallas kernels for 0%

commit v1 on v0

v1 whole, which is shorter than its diff:
```python
import functools

import jax
import jax.numpy as jnp
from jax import lax
from jax.experimental import pallas as pl
from jax.experimental.pallas import tpu as pltpu
from jax.sharding import PartitionSpec as P

MESH = pl.DeviceIdType.MESH
F32, BF16 = jnp.float32, jnp.bfloat16
NT = (((1,), (1,)), ((), ()))
TN = (((0,), (0,)), ((), ()))

CSRC = 8
GROUPS = 32
HALF = 16
ROWS = HALF * CSRC
WIDTH = 896
TWIDE = 8
SCALE = 2.0
DZ = (0, 1, 7, 2, 6, 3, 5, 4)

N_A, N_B = 9, 7
A1, A2, B1, B2 = (0, 5), (5, 4), (9, 4), (13, 3)
A, B = (0, N_A), (N_A, N_B)


def dot(a, b, dims=(((1,), (0,)), ((), ()))):
    return lax.dot_general(a, b, dims, preferred_element_type=F32)


def kernel(
    tok, grad, routes, weights, wg_hbm, wu_hbm, wd_hbm, lead, trail,
    out, lead_out, trail_out,
    wg, wu, wd, held, sendbuf, acc_g, acc_u, acc_d, hid, dgate, dup, probe,
    low_mine, low_all, x2s, to_r, to_l, to_y, x2_l, x2_r, from_l, from_r, from_y, own_sum,
    ret_out, ret_in, pick,
    w_sem, a2a_s, a2a_r, b_s, b_r, ag_s, ag_r, rs_s, rs_r, low_s, low_r, ret_s, ret_r, loc_sem,
):
    e = lax.axis_index("expert")
    t = lax.axis_index("tensor")
    z, yl, c = e // 4, (e // 2) % 2, e % 2
    yh, x = t // 4, t % 4
    xr, xl, x2, yo = (x + 1) % 4, (x + 3) % 4, (x + 2) % 4, 1 - yh
    to_right, to_left, across = (e, yh * 4 + xr), (e, yh * 4 + xl), (e, yo * 4 + x)
    col = {"o": x, "r": xr, "l": xl, "2": x2}
    ch = {k: yh * 4 + v for k, v in col.items()}
    ch.update({"p" + k: yo * 4 + v for k, v in col.items()})

    def expert_at(p, sign):
        dz, dyl, dc = DZ[p // 4], (p // 2) % 2, p % 2
        zz = (z + (dz if sign > 0 else 8 - dz)) % 8
        yy = 1 - yl if dyl else yl
        cc = 1 - c if dc else c
        return (zz * 4 + yy * 2 + cc, t)

    peers = [(e, (t + k) % TWIDE) for k in range(1, TWIDE)]

    w_copies = [
        pltpu.make_async_copy(wg_hbm.at[0], wg, w_sem.at[0]),
        pltpu.make_async_copy(wu_hbm.at[0], wu, w_sem.at[1]),
    ]
    for j in range(TWIDE):
        w_copies.append(
            pltpu.make_async_copy(
                wd_hbm.at[0, :, pl.ds(j * WIDTH, WIDTH)], wd.at[j, pl.ds(0, 304)], w_sem.at[2 + j]
            )
        )
    w_copies.append(
        pltpu.make_async_copy(trail.at[0], wd.at[t, pl.ds(304, 16)], w_sem.at[10])
    )

    barrier = pltpu.get_barrier_semaphore()
    for p in range(1, GROUPS):
        pl.semaphore_signal(barrier, inc=1, device_id=expert_at(p, 1), device_id_type=MESH)
    for peer in peers:
        pl.semaphore_signal(barrier, inc=1, device_id=peer, device_id_type=MESH)
    for cp in w_copies:
        cp.start()

    r = routes[...]
    experts = lax.broadcasted_iota(jnp.int32, (64, GROUPS), 1)
    hot = [(r[:, k : k + 1] == experts).astype(F32) for k in range(2)]
    lower = (
        lax.broadcasted_iota(jnp.int32, (64, 64), 0) > lax.broadcasted_iota(jnp.int32, (64, 64), 1)
    ).astype(BF16)
    earlier = dot(lower, (hot[0] + hot[1]).astype(BF16))
    lanes = lax.broadcasted_iota(jnp.int32, (64, GROUPS * CSRC), 1)
    picks, scaled = [], []
    grads = grad[...].astype(F32)
    for k in range(2):
        rk = r[:, k : k + 1]
        dz = ((rk >> 2) - z) & 7
        near = jnp.where(dz == 0, 0, jnp.where(dz <= 4, 2 * dz - 1, 16 - 2 * dz))
        place = near * 4 + (((rk >> 1) & 1) ^ yl) * 2 + ((rk & 1) ^ c)
        slot = jnp.sum(earlier * hot[k], axis=1, keepdims=True).astype(jnp.int32)
        picks.append(((place * CSRC + slot) == lanes).astype(F32))
        scaled.append((weights[:, k : k + 1] * grads).astype(BF16))
    both = (picks[0] + picks[1]).astype(BF16)
    pick[...] = both
    xs = dot(both, tok[...], TN)
    gs = dot(picks[0].astype(BF16), scaled[0], TN) + dot(picks[1].astype(BF16), scaled[1], TN)
    packed = jnp.concatenate(
        [xs.reshape(GROUPS, CSRC, WIDTH), gs.reshape(GROUPS, CSRC, WIDTH)], axis=1
    ).astype(BF16)
    sendbuf[...] = packed

    pl.semaphore_wait(barrier, GROUPS - 1 + len(peers))

    started = []

    def remote(src, dst, ss, rs, dev):
        return pltpu.make_async_remote_copy(
            src_ref=src, dst_ref=dst, send_sem=ss, recv_sem=rs, device_id=dev, device_id_type=MESH
        )

    def send(*args):
        cp = remote(*args)
        cp.start()
        started.append(cp)

    def arrive(dst, ss, rs):
        remote(dst, dst, ss, rs, to_right).wait_recv()

    own_copy = pltpu.make_async_copy(sendbuf.at[0], held.at[t, 0], loc_sem.at[0])
    own_copy.start()
    for p in range(1, GROUPS):
        send(sendbuf.at[p], held.at[t, p], a2a_s.at[p], a2a_r.at[p], expert_at(p, 1))
    for k, peer in enumerate(peers):
        send(trail.at[0], wd.at[t, pl.ds(304, 16)], b_s.at[k], b_r.at[k], peer)

    def region(name, h, part):
        return held.at[ch[name], pl.ds(h * HALF + part[0], part[1])]

    def forward(h, i, name, part, dev):
        ref = region(name, h, part)
        send(ref, ref, ag_s.at[h, i], ag_r.at[h, i], dev)

    def got(h, i, name, part):
        arrive(region(name, h, part), ag_s.at[h, i], ag_r.at[h, i])

    def products(h, name, first=False):
        j = ch[name]
        block = held[j, pl.ds(h * HALF, HALF)].astype(F32)
        xrows = block[:, :CSRC].reshape(ROWS, WIDTH).astype(BF16)
        grows = block[:, CSRC:].reshape(ROWS, WIDTH).astype(BF16)
        rows = pl.ds(pl.multiple_of(j * WIDTH, WIDTH), WIDTH)
        for acc, val in (
            (acc_g, dot(xrows, wg[rows, :])),
            (acc_u, dot(xrows, wu[rows, :])),
            (acc_d, dot(grows, wd[j], NT)),
        ):
            if first:
                acc[h] = val
            else:
                acc[h] += val

    def input_part(h, name):
        j = ch[name]
        rows = pl.ds(pl.multiple_of(j * WIDTH, WIDTH), WIDTH)
        return dot(dgate[h], wg[rows, :], NT) + dot(dup[h], wu[rows, :], NT)

    def middle(h):
        probe_h = acc_d[h][:, 304:320].astype(BF16)
        probe[h] = probe_h
        gate, up = acc_g[h], acc_u[h]
        dh = acc_d[h][:, :304] + SCALE * dot(probe_h, lead[0], NT)
        sig = jax.nn.sigmoid(gate)
        act = gate * sig
        hidden = (act * up).astype(BF16)
        hid[h] = hidden
        dgate[h] = (dh * up * sig * (1.0 + gate * (1.0 - sig))).astype(BF16)
        dup[h] = (dh * act).astype(BF16)
        low_mine[h] = jnp.transpose(dot(hidden, lead[0]))

    def half(h):
        if h == 0:
            own_copy.wait()
        for p in range(max(1, h * HALF), (h + 1) * HALF):
            arrive(held.at[t, p], a2a_s.at[p], a2a_r.at[p])
        forward(h, 0, "o", A, across)
        forward(h, 1, "o", B, to_right)
        forward(h, 2, "o", B, to_left)
        forward(h, 4, "o", A, to_right)
        forward(h, 5, "o", A, to_left)
        forward(h, 3, "o", B, across)
        yield
        if h == 0:
            for cp in w_copies:
                cp.wait()
        products(h, "o", first=True)
        yield
        got(h, 1, "l", B)
        forward(h, 6, "l", B1, to_right)
        forward(h, 8, "l", B, across)
        got(h, 2, "r", B)
        forward(h, 7, "r", B2, to_left)
        forward(h, 9, "r", B, across)
        got(h, 0, "po", A)
        forward(h, 14, "po", A, to_right)
        forward(h, 15, "po", A, to_left)
        yield
        got(h, 4, "l", A)
        forward(h, 12, "l", A1, to_right)
        got(h, 5, "r", A)
        forward(h, 13, "r", A2, to_left)
        yield
        if h == 0:
            for k in range(TWIDE - 1):
                arrive(wd.at[(t + TWIDE - 1 - k) % TWIDE, pl.ds(304, 16)], b_s.at[k], b_r.at[k])
        products(h, "l")
        yield
        got(h, 6, "2", B1)
        forward(h, 10, "2", B1, across)
        got(h, 7, "2", B2)
        forward(h, 11, "2", B2, across)
        yield
        products(h, "r")
        yield
        got(h, 14, "pl", A)
        forward(h, 16, "pl", A1, to_right)
        got(h, 15, "pr", A)
        forward(h, 17, "pr", A2, to_left)
        yield
        got(h, 12, "2", A1)
        got(h, 13, "2", A2)
        products(h, "2")
        yield
        got(h, 3, "po", B)
        products(h, "po")
        yield
        got(h, 8, "pl", B)
        products(h, "pl")
        yield
        got(h, 9, "pr", B)
        products(h, "pr")
        yield
        got(h, 16, "p2", A1)
        got(h, 17, "p2", A2)
        got(h, 10, "p2", B1)
        got(h, 11, "p2", B2)
        products(h, "p2")
        yield
        middle(h)
        yield
        for s, row in ((1, "p"), (0, "")):
            x2s[h, s] = input_part(h, row + "2").astype(BF16)
            send(x2s.at[h, s, pl.ds(0, 64)], x2_l.at[h, s], rs_s.at[h, s, 0], rs_r.at[h, s, 0], to_right)
            send(x2s.at[h, s, pl.ds(64, 64)], x2_r.at[h, s], rs_s.at[h, s, 1], rs_r.at[h, s, 1], to_left)
            yield
        for k, peer in enumerate(peers):
            send(low_mine.at[h], low_all.at[h, k], low_s.at[h, k], low_r.at[h, k], peer)
        for s, row in ((1, "p"), (0, "")):
            part = input_part(h, row + "r")
            arrive(x2_l.at[h, s], rs_s.at[h, s, 0], rs_r.at[h, s, 0])
            to_r[h, s] = jnp.concatenate(
                [part[:64] + x2_l[h, s].astype(F32), part[64:]], axis=0
            ).astype(BF16)
            send(to_r.at[h, s], from_l.at[h, s], rs_s.at[h, s, 2], rs_r.at[h, s, 2], to_right)
            yield
            part = input_part(h, row + "l")
            arrive(x2_r.at[h, s], rs_s.at[h, s, 1], rs_r.at[h, s, 1])
            to_l[h, s] = jnp.concatenate(
                [part[:64], part[64:] + x2_r[h, s].astype(F32)], axis=0
            ).astype(BF16)
            send(to_l.at[h, s], from_r.at[h, s], rs_s.at[h, s, 3], rs_r.at[h, s, 3], to_left)
            yield
        own_sum[1] = input_part(h, "po")
        own_sum[0] = input_part(h, "o")
        for s in (1, 0):
            arrive(from_l.at[h, s], rs_s.at[h, s, 2], rs_r.at[h, s, 2])
            arrive(from_r.at[h, s], rs_s.at[h, s, 3], rs_r.at[h, s, 3])
            total = own_sum[s] + from_l[h, s].astype(F32) + from_r[h, s].astype(F32)
            if s:
                to_y[h] = total.astype(BF16)
                send(to_y.at[h], from_y.at[h], rs_s.at[h, s, 4], rs_r.at[h, s, 4], across)
            else:
                own_sum[0] = total
        arrive(from_y.at[h], rs_s.at[h, 1, 4], rs_r.at[h, 1, 4])
        final = (own_sum[0] + from_y[h].astype(F32)).reshape(HALF, CSRC, WIDTH)
        ret_out[pl.ds(h * HALF, HALF)] = jnp.concatenate(
            [final[:, :, :512], final[:, :, 384:]], axis=1
        ).astype(BF16)
        for p in range(max(1, h * HALF), (h + 1) * HALF):
            send(ret_out.at[p], ret_in.at[p], ret_s.at[p], ret_r.at[p], expert_at(p, -1))
        yield

    order = [0] * 9 + [1] * 1 + [0] * 4 + [1] * 2 + [0] * 2
    order += [1, 0, 1, 0, 1, 0, 1, 0, 1, 0, 1, 0]
    gens = [half(0), half(1)]
    for h in order:
        next(gens[h], None)
    for g in gens:
        for _ in g:
            pass

    lead_out[0] = SCALE * (dot(hid[0], probe[0], TN) + dot(hid[1], probe[1], TN))
    own = held[t].astype(F32)
    trail_sum = jnp.zeros((16, WIDTH), F32)
    for h in range(2):
        low = low_mine[h]
        for k in range(TWIDE - 1):
            arrive(low_all.at[h, k], low_s.at[h, k], low_r.at[h, k])
            low = low + low_all[h, k]
        grows = own[h * HALF : (h + 1) * HALF, CSRC:].reshape(ROWS, WIDTH).astype(BF16)
        trail_sum = trail_sum + dot(low.astype(BF16), grows)
    trail_out[0] = SCALE * trail_sum

    for p in range(1, GROUPS):
        arrive(ret_in.at[p], ret_s.at[p], ret_r.at[p])
    ret_in[0] = ret_out[0]
    back = ret_in[...].astype(F32)
    first = back[:, :CSRC].reshape(GROUPS * CSRC, 512).astype(BF16)
    last = back[:, CSRC:].reshape(GROUPS * CSRC, 512).astype(BF16)
    out[:, 0:512] = dot(pick[...], first).astype(BF16)
    out[:, 512:WIDTH] = dot(pick[...], last)[:, 128:].astype(BF16)

    for cp in started:
        cp.wait_send()


def on_device(tok, grad, routes, weights, wg, wu, wd, lead, trail):
    vm = pl.BlockSpec(memory_space=pltpu.VMEM)
    hbm = pl.BlockSpec(memory_space=pl.ANY)
    dma = pltpu.SemaphoreType.DMA
    return pl.pallas_call(
        kernel,
        out_shape=(
            jax.ShapeDtypeStruct((64, WIDTH), BF16),
            jax.ShapeDtypeStruct((1, 304, 16), F32),
            jax.ShapeDtypeStruct((1, 16, WIDTH), F32),
        ),
        in_specs=[vm, vm, vm, vm, hbm, hbm, hbm, vm, vm],
        out_specs=(vm, vm, vm),
        scratch_shapes=[
            pltpu.VMEM((7168, 304), BF16),
            pltpu.VMEM((7168, 304), BF16),
            pltpu.VMEM((TWIDE, 320, WIDTH), BF16),
            pltpu.VMEM((TWIDE, GROUPS, 16, WIDTH), BF16),
            pltpu.VMEM((GROUPS, 16, WIDTH), BF16),
            pltpu.VMEM((2, ROWS, 304), F32),
            pltpu.VMEM((2, ROWS, 304), F32),
            pltpu.VMEM((2, ROWS, 320), F32),
            pltpu.VMEM((2, ROWS, 304), BF16),
            pltpu.VMEM((2, ROWS, 304), BF16),
            pltpu.VMEM((2, ROWS, 304), BF16),
            pltpu.VMEM((2, ROWS, 16), BF16),
            pltpu.VMEM((2, 16, ROWS), F32),
            pltpu.VMEM((2, TWIDE - 1, 16, ROWS), F32),
            pltpu.VMEM((2, 2, ROWS, WIDTH), BF16),
            pltpu.VMEM((2, 2, ROWS, WIDTH), BF16),
            pltpu.VMEM((2, 2, ROWS, WIDTH), BF16),
            pltpu.VMEM((2, ROWS, WIDTH), BF16),
            pltpu.VMEM((2, 2, 64, WIDTH), BF16),
            pltpu.VMEM((2, 2, 64, WIDTH), BF16),
            pltpu.VMEM((2, 2, ROWS, WIDTH), BF16),
            pltpu.VMEM((2, 2, ROWS, WIDTH), BF16),
            pltpu.VMEM((2, ROWS, WIDTH), BF16),
            pltpu.VMEM((2, ROWS, WIDTH), F32),
            pltpu.VMEM((GROUPS, 16, 512), BF16),
            pltpu.VMEM((GROUPS, 16, 512), BF16),
            pltpu.VMEM((64, GROUPS * CSRC), BF16),
            dma((11,)),
            dma((GROUPS,)),
            dma((GROUPS,)),
            dma((TWIDE - 1,)),
            dma((TWIDE - 1,)),
            dma((2, 18)),
            dma((2, 18)),
            dma((2, 2, 5)),
            dma((2, 2, 5)),
            dma((2, TWIDE - 1)),
            dma((2, TWIDE - 1)),
            dma((GROUPS,)),
            dma((GROUPS,)),
            dma((1,)),
        ],
        compiler_params=pltpu.CompilerParams(
            collective_id=0, has_side_effects=True, vmem_limit_bytes=56 * 1024 * 1024
        ),
        cost_estimate=pl.CostEstimate(
            flops=6_000_000_000, bytes_accessed=16_000_000, transcendentals=80_000
        ),
    )(tok, grad, routes, weights, wg, wu, wd, lead, trail)


def solution(mesh):
    placed = (
        P("expert", "tensor"),
        P("expert", "tensor"),
        P("expert", None),
        P("expert", None),
        P("expert", None, "tensor"),
        P("expert", None, "tensor"),
        P("expert", "tensor", None),
        P("expert", "tensor", None),
        P("expert", None, "tensor"),
    )
    return jax.shard_map(
        on_device,
        mesh=mesh,
        in_specs=placed,
        out_specs=(P("expert", "tensor"), P("expert", "tensor", None), P("expert", None, "tensor")),
        check_vma=False,
    )
```

time: 435 us -> 152 us (0.35)
  waiting for transfers between devices: 209 us -> 0 us
  Pallas kernels: 0 us -> 126 us
  blocking collectives: 101 us -> 0 us
  starting transfers between devices: 30.8 us -> 0 us
  matrix products: 23.6 us -> 0 us
  local copies, waits for them, and re-layouts: 46.1 us -> 23.7 us
  between operations: 14.3 us -> 0.64 us
  other arithmetic: 8.88 us -> 0 us
    pallas_call x0 -> x1, Pallas kernels: none -> 126 us  [on_device(): pl.pallas_call(kernel, out_shape=(jax.ShapeDtypeStruct((64, WIDTH), BF16)...]
    all_to_all x3 -> x0, waiting for transfers between devices: 125 us -> none  [the longest x1 76.9 us: on_device(): lax.all_to_all(g_buf, 'expert', split_axis=0, concat_axis=0, tiled=True)]
    unnamed x2 -> x0, waiting for transfers between devices: 84.9 us -> none
    all_gather x2 -> x0, blocking collectives: 64.8 us -> none  [the longest x1 32.9 us: on_device(): lax.all_gather(layer_output_gradient, 'tensor', axis=1, tiled=True)]
    psum x1 -> x0, blocking collectives: 36.1 us -> none  [on_device(): lax.psum(probe_partial.astype(jnp.bfloat16), 'tensor').astype(jnp.float32)]
    all_to_all x3 -> x0, starting transfers between devices: 30.8 us -> none  [the longest x1 15.5 us: on_device(): lax.all_to_all(x_buf, 'expert', split_axis=0, concat_axis=0, tiled=True)]
    dot_general x10 -> x0, matrix products: 23.6 us -> none  [the longest x1 4.81 us: on_device(): jnp.einsum('erd,edf->erf', x_rows, gating_projection, preferred_element_t...]
    mul x5 -> x0, local copies, waits for them, and re-layouts: 8.83 us -> none  [the longest x3 8.59 us: on_device(): router_weight_pair[:, :, None] * full_grad[:, None, :].astype(jnp.float32)]
  transfers between devices with their start and end apart: 4 -> 0, of which waited for: 4 -> 0; matrix products, arithmetic and copies ran while one was open for 6% -> 0% of each run, Pallas kernels for 0% -> 0%
where the time goes in v1:
time: 152 us; the launch traced here: 151 us
  Pallas kernels  126 us (83%)
  local copies, waits for them, and re-layouts  23.7 us (16%)
    pallas_call x1, Pallas kernels, on_device(): pl.pallas_call(kernel, out_shape=(jax.ShapeDtypeStruct((64, WIDTH), BF16)...  126 us
    unnamed x7, local copies, waits for them, and re-layouts  22.1 us

profile of v1, /device:TPU:1, one launch (start us, length us, event | category | flops | bytes accessed | tf_op | source)
XLA Modules:
  0.0 150.7 jit_solution(14583721401845459366)
XLA Ops:
  0.6 1.4 copy.12.routes
  2.0 1.4 copy.13.weights
  3.4 1.4 copy.16.lead
  4.8 7.4 %copy.14.wg_hbm = bf16[1,7168,304]{2,1,0:T(8,128)(2,1)} copy(bf16[1,7168,304]{1,2,0:T(8,128)(2,1)} %param.13) | data formatting | bytes 8716288 | tf_op args[4]
  12.3 7.4 %copy.15.wu_hbm = bf16[1,7168,304]{2,1,0:T(8,128)(2,1)} copy(bf16[1,7168,304]{1,2,0:T(8,128)(2,1)} %param.14) | data formatting | bytes 8716288 | tf_op args[5]
  19.7 126.3 %shard_map.112 = (bf16[64,896]{1,0:T(8,128)(2,1)}, f32[1,304,16]{2,1,0:T(8,128)}, f32[1,16,896]{2,1,0:T(8,128)}) custom-call(bf16[64,896]{1,0:T(8,128)(2,1)} %tok.1, bf16[64,896]{1,0:T(8,128)(2,1)} %grad.1, s32[64,2]{1,0:T(8,128)} %copy.12.routes, f32[64,2]{1,0:T(8,128)} %copy.13.weights, bf16[1,7168,304]{2,1,0:T(8,128)(2,1)} %copy.14.wg_hbm, ...), custom_call_target="tpu_custom_call" | custom-call | flops 6000000000 | bytes 16000000 | tf_op jit(solution)/shard_map/pallas_call | solution.py:327
  146.0 1.6 %copy.17 = f32[1,304,16]{1,2,0:T(8,128)} copy(f32[1,304,16]{2,1,0:T(8,128)} %get-tuple-element.4) | data formatting | bytes 38912 | tf_op jit(solution)/shard_map/pallas_call | solution.py:327
  147.7 1.6 %copy.20 = bf16[64,896]{1,0:T(8,128)(2,1)} copy(bf16[64,896]{1,0:T(8,128)(2,1)} %get-tuple-element.9) | data formatting | bytes 229376
  149.2 1.4 copy.21
